TPU v7x, 32 devices: a whole 2x2x4 slice. The times are simulated.
32 devices in a mesh: groups: 2 (over y), ctx: 8 (over z, x), head: 2 (over core).
Axes of the slice: x: 2, y: 2, z: 4, core: 2. Of those that a mesh axis runs over, the one named last changes fastest.
Arguments:
- queries: bfloat16 [4096, 2, 256], P(('groups', 'ctx'), 'head'), parts along dimension 0, may hold values from -6 to 6
- keys: bfloat16 [4096, 2, 256], P(('groups', 'ctx'), 'head'), parts along dimension 0, may hold values from -6 to 6
- values: bfloat16 [4096, 2, 256], P(('groups', 'ctx'), 'head'), parts along dimension 0, may hold values from -6 to 6
- lambda_vectors: float32 [4, 2, 128], P(None, 'head'), may hold values from -1.2 to 1.2
- out_weight: bfloat16 [8192, 512], P('ctx', 'head'), may hold values from -0.25 to 0.25
- local_len: int32 [32], P(('groups', 'ctx')), parts along dimension 0, may hold values from 1 to 3
- stride_keys: int32 [32, 3], P(('groups', 'ctx')), parts along dimension 0, may hold values from -1 to 11, as said below
- global_blocks: int32 [8], P('groups'), parts along dimension 0, may hold values from 0 to 15, as said below
Outputs:
- layer_out: bfloat16 [4096, 8192], P(('groups', 'ctx'), 'head'), parts along dimension 0
There are 2 independent parts, one for each index of `groups`. A program takes and returns all parts, laid end to end along the dimension named above; an argument that names none is the same for every part. Nothing has to cross between parts.
Inputs may be any that keep to these rules, and one draw needn't show every extreme that they name: `stride_keys`: entry j of query block b is either b - (j + 1) * 4 or -1, and -1 where that would be negative. `global_blocks`: 4 distinct block indices.
All inputs are finite; a program needn't handle non-finite values.
Results may differ from a plain program's by a relative error of at most 0.001.
The roundings to bfloat16 on the way count: a program that leaves them out, or rounds other values in their place, can miss the bound.
Values may be sent and summed in bfloat16 or wider, within the bound.
A program may use at most 64 MiB of HBM per device.

v0:
```python
import math

import jax
import jax.numpy as jnp
from jax import lax
from jax.sharding import PartitionSpec as P

BLK = 128
NSTR = 3
GLOB = 4
LAYER = 12


def shifted(shard, axis, by):
    length = lax.axis_size(axis)
    pairs = [(i, i + by) for i in range(length) if 0 <= i + by < length]
    return lax.ppermute(shard, axis, pairs)


def from_root(value, axis, source):
    kept = jnp.where(lax.axis_index(axis) == source, value, 0).astype(value.dtype)
    return lax.psum(kept, axis)


def masked_softmax(scores, allowed):
    masked_scores = jnp.where(allowed, scores, -jnp.inf)
    highest = jnp.max(masked_scores, -1, keepdims=True)
    raised = jnp.where(allowed, jnp.exp(masked_scores - highest), 0.0)
    return raised / jnp.sum(raised, -1, keepdims=True)


def body(queries, keys, values, lambda_vectors, out_weight, local_len, stride_keys, global_blocks):
    tok_dev, heads_here, double_width = queries.shape
    head_dim = double_width // 2
    blocks_here = tok_dev // BLK
    ctx_count = lax.axis_size("ctx")
    ctx_pos = lax.axis_index("ctx")
    step_dev = ctx_count // (NSTR + 1)
    lam_init = 0.8 - 0.6 * math.exp(-0.3 * (LAYER - 1))
    mixing = (
        jnp.exp(jnp.sum(lambda_vectors[0] * lambda_vectors[1], -1))
        - jnp.exp(jnp.sum(lambda_vectors[2] * lambda_vectors[3], -1))
        + lam_init
    )
    key_vals = jnp.concatenate((keys, values), axis=-1)
    prev_data = shifted(key_vals, "ctx", 1)
    remote = []
    moving = key_vals
    for slot_pos in range(NSTR):
        moving = shifted(moving, "ctx", step_dev)
        remote.append(moving)
    global_list = []
    for global_pos in range(GLOB):
        block_id = global_blocks[global_pos]
        owner_pos = block_id // blocks_here
        first_row = block_id % blocks_here * BLK
        block_data = lax.dynamic_slice_in_dim(key_vals, first_row, BLK, 0)
        global_list.append(from_root(block_data, "ctx", owner_pos))
    global_data = jnp.concatenate(global_list, 0)
    candidates = jnp.concatenate([key_vals, prev_data] + remote + [global_data], 0)
    cand_keys = candidates[..., :double_width]
    cand_values = candidates[..., double_width:]
    rows_here = jnp.arange(tok_dev, dtype=jnp.int32)
    query_pos = ctx_pos * tok_dev + rows_here
    query_block = query_pos // BLK
    owner_mask = (rows_here // BLK)[:, None] == jnp.arange(blocks_here, dtype=jnp.int32)[None, :]
    length = jnp.sum(jnp.where(owner_mask, local_len[None, :], 0), 1)
    stride_rows = jnp.sum(jnp.where(owner_mask[:, :, None], stride_keys[None, :, :], 0), 1)
    window_floor = query_block - length
    own_block = ctx_pos * blocks_here + rows_here // BLK
    own_ok = (own_block[None, :] > window_floor[:, None]) & (
        query_pos[None, :] - rows_here[:, None] + rows_here[None, :] <= query_pos[:, None]
    )
    prev_block = (ctx_pos - 1) * blocks_here + rows_here // BLK
    prev_ok = (prev_block[None, :] > window_floor[:, None]) & (prev_block[None, :] >= 0)
    masks = [own_ok, prev_ok]
    for slot_pos in range(NSTR):
        far_block = (ctx_pos - (slot_pos + 1) * step_dev) * blocks_here + rows_here // BLK
        listed = stride_rows[:, slot_pos][:, None]
        masks.append((listed == far_block[None, :]) & (listed >= 0))
    in_stride = jnp.any(stride_rows[:, :, None] == global_blocks[None, None, :], 1)
    global_key = jnp.repeat(global_blocks, BLK)
    global_ok = (global_key[None, :] <= window_floor[:, None]) & jnp.logical_not(
        jnp.repeat(in_stride, BLK, axis=1)
    )
    masks.append(global_ok)
    allowed = jnp.concatenate(masks, 1)
    score_scale = 1.0 / math.sqrt(head_dim)
    scores_one = (
        jnp.einsum(
            "qhd,khd->hqk",
            queries[..., :head_dim],
            cand_keys[..., :head_dim],
            preferred_element_type=jnp.float32,
        )
        * score_scale
    )
    scores_two = (
        jnp.einsum(
            "qhd,khd->hqk",
            queries[..., head_dim:],
            cand_keys[..., head_dim:],
            preferred_element_type=jnp.float32,
        )
        * score_scale
    )
    attn_one = masked_softmax(scores_one, allowed)
    attn_two = masked_softmax(scores_two, allowed)
    weights = (attn_one - mixing[:, None, None] * attn_two).astype(jnp.bfloat16)
    mixed_out = jnp.einsum("hqk,khe->qhe", weights, cand_values, preferred_element_type=jnp.float32)
    normed = (
        mixed_out
        * lax.rsqrt(jnp.mean(mixed_out * mixed_out, -1, keepdims=True) + 1e-05)
        * (1.0 - lam_init)
    ).astype(jnp.bfloat16)
    flat_heads = normed.reshape(tok_dev, heads_here * double_width)
    partials = lax.dot_general(
        flat_heads,
        lax.all_gather(out_weight, "ctx", axis=0, tiled=True),
        (((1,), (1,)), ((), ())),
        preferred_element_type=jnp.float32,
    )
    return lax.psum_scatter(partials.astype(jnp.bfloat16), "head", scatter_dimension=1, tiled=True)


def solution(mesh):
    in_specs = (
        P(("groups", "ctx"), "head", None),
        P(("groups", "ctx"), "head", None),
        P(("groups", "ctx"), "head", None),
        P(None, "head", None),
        P("ctx", "head"),
        P(("groups", "ctx")),
        P(("groups", "ctx"), None),
        P("groups"),
    )
    out_specs = P(("groups", "ctx"), "head")
    return jax.shard_map(body, mesh=mesh, in_specs=in_specs, out_specs=out_specs, check_vma=False)
```

profile of v0, /device:TPU:24, one launch (start us, length us, event | category | flops | bytes accessed | tf_op | source)
XLA Modules:
  0.0 195.6 jit_solution(15763961932910393924)
XLA Ops:
  6.5 0.0 copy-start
  6.5 0.0 copy-start.2
  6.5 0.0 copy-start.3
  6.5 0.0 copy-start.1
  6.5 0.0 all-reduce.3.cloned.1.call-start
  6.6 1.5 fusion.21
  18.3 0.9 constant_dynamic-update-slice_fusion.1
  19.3 0.9 constant_dynamic-update-slice_fusion
  20.2 0.8 dynamic-slice_select_fusion
  21.0 0.0 all-reduce.3.cloned.1.call-update
  21.0 0.0 all-gather.2.cloned.1.call-start
  21.1 0.7 all-gather.2.cloned.1.call-update
  21.8 0.0 reduce-scatter.2.cloned.1.call-start
  21.8 3.4 %collective-permute-start = (bf16[256,1,512]{2,0,1:T(8,128)(2,1)S(1)}, bf16[256,1,512]{2,0,1:T(8,128)(2,1)S(1)}, u32[]{:S(2)}, u32[]{:S(2)}) collective-permute-start(bf16[256,1,512]{2,0,1:T(8,128)(2,1)S(1)} %get-tuple-element.20), channel_id=1, source_target_pairs={{0,2},{2,4},{4,6},{6,8},{8,10},{10,12},{12,14},{1,3},{3,5},{5,7},{... | collective-permute-start | bytes 786440 | tf_op jit(solution)/shard_map/ppermute | solution.py:17
  25.3 1.3 collective-permute-start.1
  26.6 0.0 copy-done.2
  26.6 0.1 copy.10
  26.7 0.1 select_reduce_fusion
  26.8 0.0 copy-done.3
  26.8 0.1 select_reduce_fusion.1
  26.9 0.0 copy-done
  26.9 0.1 compare_reduce_fusion
  27.0 0.1 broadcast_bitcast_fusion
  27.1 0.0 copy-start.4
  27.1 0.1 fusion.7
  27.3 0.2 and_dynamic-update-slice_fusion.3
  27.4 0.1 and_dynamic-update-slice_fusion.2
  27.6 0.1 and_dynamic-update-slice_fusion.1
  27.7 12.6 %collective-permute-done.1 = bf16[256,1,512]{2,0,1:T(8,128)(2,1)S(1)} collective-permute-done((bf16[256,1,512]{2,0,1:T(8,128)(2,1)S(1)}, bf16[256,1,512]{2,0,1:T(8,128)(2,1)S(1)}, u32[]{:S(2)}, u32[]{:S(2)}) %collective-permute-start.1) | collective-permute-done | bytes 262176 | tf_op jit(solution)/shard_map/ppermute | solution.py:17
  40.4 1.3 collective-permute-start.2
  41.6 0.0 copy-done.1
  41.7 0.7 multiply_reduce_fusion.1
  43.7 0.1 and_dynamic-update-slice_fusion
  43.8 0.2 constant_dynamic-update-slice_fusion.12
  44.0 6.7 %collective-permute-done.2 = bf16[256,1,512]{2,0,1:T(8,128)(2,1)S(1)} collective-permute-done((bf16[256,1,512]{2,0,1:T(8,128)(2,1)S(1)}, bf16[256,1,512]{2,0,1:T(8,128)(2,1)S(1)}, u32[]{:S(2)}, u32[]{:S(2)}) %collective-permute-start.2) | collective-permute-done | bytes 262176 | tf_op jit(solution)/shard_map/ppermute | solution.py:17
  50.7 1.3 collective-permute-start.3
  52.0 0.0 collective-permute-done
  52.1 8.1 %collective-permute-done.3 = bf16[256,1,512]{2,0,1:T(8,128)(2,1)S(1)} collective-permute-done((bf16[256,1,512]{2,0,1:T(8,128)(2,1)S(1)}, bf16[256,1,512]{2,0,1:T(8,128)(2,1)S(1)}, u32[]{:S(2)}, u32[]{:S(2)}) %collective-permute-start.3) | collective-permute-done | bytes 262176 | tf_op jit(solution)/shard_map/ppermute | solution.py:17
  60.2 36.6 %all-reduce.3.cloned.1.call-done = (bf16[128,1,512]{2,0,1:T(8,128)(2,1)}, bf16[128,1,512]{2,0,1:T(8,128)(2,1)}, bf16[128,1,512]{2,0,1:T(8,128)(2,1)}, bf16[128,1,512]{2,0,1:T(8,128)(2,1)}) async-done(((bf16[128,1,512]{2,0,1:T(8,128)(2,1)}, bf16[128,1,512]{2,0,1:T(8,128)(2,1)}, bf16[128,1,512]{2,0,1:T(8,128)(2,1)}, bf16[128,1,512]{2,0,1:T(8,128)(2,1)}), (bf16[128,1,512]{2,0,1:T(8,128)(2,1)}, ...) | async-done | bytes 524304 | tf_op jit(solution)/shard_map/psum | solution.py:22
  96.8 0.9 constant_dynamic-update-slice_fusion.5
  97.7 0.9 constant_dynamic-update-slice_fusion.4
  98.6 0.9 constant_dynamic-update-slice_fusion.3
  99.6 0.9 constant_dynamic-update-slice_fusion.2
  100.5 0.0 copy-done.4
  100.5 0.5 fusion.23
  101.0 0.5 fusion.22
  101.5 0.8 fusion.4
  102.2 1.1 multiply_reduce_fusion
  103.4 67.6 %all-gather.2.cloned.1.call-done = bf16[8192,256]{1,0:T(8,128)(2,1)} async-done(((bf16[1024,256]{1,0:T(8,128)(2,1)}), bf16[8192,256]{1,0:T(8,128)(2,1)}) %all-gather.2.cloned.1.call-update) | async-done | bytes 4194320 | tf_op jit(solution)/shard_map/all_gather | solution.py:119
  171.0 5.5 %convolution_convert_fusion = bf16[256,8192]{1,0:T(8,128)(2,1)} fusion(bf16[8192,256]{1,0:T(8,128)(2,1)} %all-gather.2.cloned.1.call-done, f32[1,256,256]{2,1,0:T(8,128)S(1)} %get-tuple-element.36, f32[256]{0:T(256)S(1)} %add_rsqrt_fusion), kind=kOutput, calls=%fused_computation | convolution fusion | flops 1076035584 | bytes 8651776 | tf_op jit(solution)/shard_map/dot_general | solution.py:117
  176.4 0.0 reduce-scatter.2.cloned.1.call-update
  176.5 12.6 %reduce-scatter.2.cloned.1.call-done = bf16[256,4096]{1,0:T(8,128)(2,1)} async-done(((bf16[256,8192]{1,0:T(8,128)(2,1)}), bf16[256,4096]{1,0:T(8,128)(2,1)}) %reduce-scatter.2.cloned.1.call-update) | async-done | bytes 2097168 | tf_op jit(solution)/shard_map/reduce_scatter | solution.py:123
  (15 shorter events, 0.2 us)
Async XLA Ops:
  6.5 20.4 %copy-start = (s32[4]{0:T(128)S(1)}, s32[4]{0:T(128)}, u32[]{:S(2)}) copy-start(s32[4]{0:T(128)} %param.15) | copy-start | bytes 52
  6.5 20.0 %copy-start.2 = (s32[2,3]{1,0:T(2,128)S(1)}, s32[2,3]{1,0:T(2,128)}, u32[]{:S(2)}) copy-start(s32[2,3]{1,0:T(2,128)} %param.14) | copy-start | bytes 76
  6.5 20.3 %copy-start.3 = (s32[2]{0:T(128)S(1)}, s32[2]{0:T(128)}, u32[]{:S(2)}) copy-start(s32[2]{0:T(128)} %param.13) | copy-start | bytes 28
  6.5 35.1 %copy-start.1 = (f32[4,1,128]{2,1,0:T(1,128)S(1)}, f32[4,1,128]{2,1,0:T(1,128)}, u32[]{:S(2)}) copy-start(f32[4,1,128]{2,1,0:T(1,128)} %param.11) | copy-start | bytes 6148
  6.5 90.3 %all-reduce.3.cloned.1.call-start = ((), (), s32[]{:S(2)}) async-start(), calls=%async_computation.3 | async-start | bytes 1048576 | tf_op jit(solution)/shard_map/psum | solution.py:22
  21.0 149.9 %all-gather.2.cloned.1.call-start = ((), (), s32[]{:S(2)}) async-start(), calls=%async_computation.1 | async-start | bytes 4718592 | tf_op jit(solution)/shard_map/all_gather | solution.py:119
  21.8 167.3 %reduce-scatter.2.cloned.1.call-start = ((), (), s32[]{:S(2)}) async-start(), calls=%async_computation.2 | async-start | bytes 6291456 | tf_op jit(solution)/shard_map/reduce_scatter | solution.py:123
  21.8 30.2 %collective-permute-start = (bf16[256,1,512]{2,0,1:T(8,128)(2,1)S(1)}, bf16[256,1,512]{2,0,1:T(8,128)(2,1)S(1)}, u32[]{:S(2)}, u32[]{:S(2)}) collective-permute-start(bf16[256,1,512]{2,0,1:T(8,128)(2,1)S(1)} %get-tuple-element.20), channel_id=1, source_target_pairs={{0,2},{2,4},{4,6},{6,8},{8,10},{10,12},{12,14},{1,3},{3,5},{5,7},{... | collective-permute-start | bytes 786440 | tf_op jit(solution)/shard_map/ppermute | solution.py:17
  25.3 15.1 %collective-permute-start.1 = (bf16[256,1,512]{2,0,1:T(8,128)(2,1)S(1)}, bf16[256,1,512]{2,0,1:T(8,128)(2,1)S(1)}, u32[]{:S(2)}, u32[]{:S(2)}) collective-permute-start(bf16[256,1,512]{2,0,1:T(8,128)(2,1)S(1)} %get-tuple-element.20), channel_id=1, source_target_pairs={{0,4},{2,6},{4,8},{6,10},{8,12},{10,14},{1,5},{3,7},{5,9},{7,11},{... | collective-permute-start | bytes 786440 | tf_op jit(solution)/shard_map/ppermute | solution.py:17
  27.1 73.4 %copy-start.4 = (bf16[256,1,256]{2,0,1:T(8,128)(2,1)S(1)}, bf16[256,1,256]{2,0,1:T(8,128)(2,1)}, u32[]{:S(2)}) copy-start(bf16[256,1,256]{2,0,1:T(8,128)(2,1)} %param.8) | copy-start | bytes 393220
  40.4 10.4 %collective-permute-start.2 = (bf16[256,1,512]{2,0,1:T(8,128)(2,1)S(1)}, bf16[256,1,512]{2,0,1:T(8,128)(2,1)S(1)}, u32[]{:S(2)}, u32[]{:S(2)}) collective-permute-start(bf16[256,1,512]{2,0,1:T(8,128)(2,1)S(1)} %collective-permute-done.1), channel_id=1, source_target_pairs={{0,4},{2,6},{4,8},{6,10},{8,12},{10,14},{1,5},{3,7},{5,9},{7,11},{... | collective-permute-start | bytes 786440 | tf_op jit(solution)/shard_map/ppermute | solution.py:17
  50.7 9.5 %collective-permute-start.3 = (bf16[256,1,512]{2,0,1:T(8,128)(2,1)S(1)}, bf16[256,1,512]{2,0,1:T(8,128)(2,1)S(1)}, u32[]{:S(2)}, u32[]{:S(2)}) collective-permute-start(bf16[256,1,512]{2,0,1:T(8,128)(2,1)S(1)} %collective-permute-done.2), channel_id=1, source_target_pairs={{0,4},{2,6},{4,8},{6,10},{8,12},{10,14},{1,5},{3,7},{5,9},{7,11},{... | collective-permute-start | bytes 786440 | tf_op jit(solution)/shard_map/ppermute | solution.py:17
Sparse Core Ops, SparseCore 0:
  21.2 75.5 all-reduce.2
  99.2 71.7 all-gather.1
  176.6 12.4 reduce-scatter.1
where the time goes:
time: 197 us; the launch traced here: 196 us
  waiting for transfers between devices  145 us (74%)
  between operations  25 us (13%)
  matrix products  7.61 us (4%)
  starting transfers between devices  7.36 us (4%)
  local copies, waits for them, and re-layouts  7.26 us (4%)
  other arithmetic  3.48 us (2%)
    all_gather x1, waiting for transfers between devices, body(): lax.all_gather(out_weight, 'ctx', axis=0, tiled=True)  67.6 us
    psum x1, waiting for transfers between devices, from_root(): return lax.psum(kept, axis)  36.6 us
    ppermute x4, waiting for transfers between devices, shifted(): return lax.ppermute(shard, axis, pairs)  27.4 us
    reduce_scatter x1, waiting for transfers between devices, body(): lax.psum_scatter(partials.astype(jnp.bfloat16), 'head', scatter_dimension...  12.6 us
    ppermute x4, starting transfers between devices, shifted(): return lax.ppermute(shard, axis, pairs)  7.25 us
    dot_general x1, matrix products, body(): lax.dot_general(flat_heads, lax.all_gather(out_weight, 'ctx', axis=0, til...  5.48 us
  transfers between devices with their start and end apart: 7, of which 6 were waited for; matrix products, arithmetic and copies ran while one was open for 4% of the time, Pallas kernels for 0%

commit v1 on v0

--- a/solution.py
+++ b/solution.py
@@ -1,8 +1,11 @@
+import functools
 import math
 
 import jax
 import jax.numpy as jnp
 from jax import lax
+from jax.experimental import pallas as pl
+from jax.experimental.pallas import tpu as pltpu
 from jax.sharding import PartitionSpec as P
 
 BLK = 128
@@ -123,6 +126,329 @@
     return lax.psum_scatter(partials.astype(jnp.bfloat16), "head", scatter_dimension=1, tiled=True)
 
 
+MESH_ID = pl.DeviceIdType.MESH
+MASKED = -1e30
+
+
+def kernel(
+    n, q_ref, k_ref, v_ref, w_ref, lam_ref, len_ref, stride_ref, glob_ref, out_ref,
+    kv, wown, wother, scores, probs, mine, theirs, obuf,
+    kvu_s, kvx_s, kv_r, wu_s, wd_s, wx_s, w_r, wy_s, wy_r, sw_s, sw_r, nm_s, nm_r, loc, out_s,
+):
+    tok, width = q_ref.shape
+    dh = width // 2
+    rows = w_ref.shape[0]
+    half = rows // 2
+    nz, nh = n // 2, n // 2
+    y, c, h = lax.axis_index("groups"), lax.axis_index("ctx"), lax.axis_index("head")
+    z, x = c // 2, c % 2
+    has_up, has_down = z + 1 < nz, z >= 1
+    up, down, side = {"ctx": c + 2}, {"ctx": c - 2}, {"ctx": c + 1 - 2 * x}
+    twin, core = {"groups": 1 - y}, {"head": 1 - h}
+    lo = pl.multiple_of(y * half, half)
+    hi = pl.multiple_of((1 - y) * half, half)
+
+    barrier = pltpu.get_barrier_semaphore()
+    for to in (side, twin, core):
+        pl.semaphore_signal(barrier, inc=1, device_id=to, device_id_type=MESH_ID)
+
+    @pl.when(has_up)
+    def _():
+        pl.semaphore_signal(barrier, inc=1, device_id=up, device_id_type=MESH_ID)
+
+    @pl.when(has_down)
+    def _():
+        pl.semaphore_signal(barrier, inc=1, device_id=down, device_id_type=MESH_ID)
+
+    load = pltpu.make_async_copy(w_ref, wown.at[c], loc)
+    load.start()
+    kv[c, 0] = k_ref[...]
+    kv[c, 1] = v_ref[...]
+    pl.semaphore_wait(barrier, 3 + has_up.astype(jnp.int32) + has_down.astype(jnp.int32))
+
+    def remote(src, dst, send, recv, to):
+        return pltpu.make_async_remote_copy(
+            src_ref=src, dst_ref=dst, send_sem=send, recv_sem=recv, device_id=to, device_id_type=MESH_ID
+        )
+
+    def kv_copy(b, send, to):
+        return remote(kv.at[b], kv.at[b], send.at[b], kv_r.at[b], to)
+
+    def w_copy(b, send, to):
+        piece = wown.at[b, pl.ds(lo, half)]
+        return remote(piece, piece, send.at[b], w_r.at[b], to)
+
+    def y_copy(b, start):
+        piece = wown.at[b, pl.ds(start, half)]
+        return remote(piece, piece, wy_s.at[b], wy_r.at[b], twin)
+
+    def swap_copy(b, which):
+        start = pl.multiple_of(which * half, half)
+        slot = b % nh
+        return remote(
+            wown.at[b, pl.ds(start, half)], wother.at[slot, pl.ds(start, half)],
+            sw_s.at[2 * slot + which], sw_r.at[2 * slot + which], core,
+        )
+
+    def swap(b, which):
+        @pl.when(b // nh == 1 - h)
+        def _():
+            swap_copy(b, which).start()
+
+    def kv_up(d):
+        @pl.when(z >= d)
+        def _():
+            b = c - 2 * d
+            kv_copy(b, kvu_s, up).wait_recv()
+
+            @pl.when(has_up)
+            def _():
+                kv_copy(b, kvu_s, up).start()
+
+            kv_copy(b, kvx_s, side).start()
+
+    def w_down(d):
+        @pl.when(z + d < nz)
+        def _():
+            b = c + 2 * d
+            w_copy(b, wd_s, down).wait_recv()
+
+            @pl.when(has_down)
+            def _():
+                w_copy(b, wd_s, down).start()
+
+            y_copy(b, lo).start()
+            w_copy(b, wx_s, side).start()
+            swap(b, y)
+
+    def w_up(d):
+        @pl.when(z >= d)
+        def _():
+            b = c - 2 * d
+            w_copy(b, wu_s, up).wait_recv()
+
+            @pl.when(has_up)
+            def _():
+                w_copy(b, wu_s, up).start()
+
+            y_copy(b, lo).start()
+            w_copy(b, wx_s, side).start()
+            swap(b, y)
+
+    def w_side(d):
+        @pl.when((z + d < nz) & (z + d >= 0))
+        def _():
+            b = 2 * (z + d) + 1 - x
+            w_copy(b, wx_s, side).wait_recv()
+            y_copy(b, lo).start()
+            swap(b, y)
+
+    def w_twin(b):
+        y_copy(b, hi).wait_recv()
+        swap(b, 1 - y)
+
+    def kv_side(d):
+        @pl.when((z >= d) & ((d > 0) | (x == 1)))
+        def _():
+            b = 2 * (z - d) + 1 - x
+            kv_copy(b, kvx_s, side).wait_recv()
+
+    @pl.when(has_up)
+    def _():
+        kv_copy(c, kvu_s, up).start()
+
+    @pl.when(x == 0)
+    def _():
+        kv_copy(c, kvx_s, side).start()
+
+    load.wait()
+
+    @pl.when(has_down)
+    def _():
+        w_copy(c, wd_s, down).start()
+
+    w_copy(c, wx_s, side).start()
+
+    @pl.when(has_up)
+    def _():
+        w_copy(c, wu_s, up).start()
+
+    swap(c, 0)
+    swap(c, 1)
+
+    for b in range(1, n):
+        @pl.when(c < b)
+        def _(b=b):
+            kv[b] = jnp.zeros(kv.shape[1:], kv.dtype)
+
+    for d in range(1, nz):
+        kv_up(d)
+        w_down(d)
+    w_side(0)
+    for d in range(1, nz):
+        w_up(d)
+        w_side(d)
+    for d in range(nz):
+        kv_side(d)
+
+    scale = 1.0 / math.sqrt(dh)
+    lam_init = 0.8 - 0.6 * math.exp(-0.3 * (LAYER - 1))
+    lam = [lam_ref[i] for i in range(4)]
+    mixing = (
+        jnp.exp(jnp.sum(lam[0] * lam[1], -1, keepdims=True))
+        - jnp.exp(jnp.sum(lam[2] * lam[3], -1, keepdims=True))
+        + lam_init
+    )
+    blocks_here = tok // BLK
+
+    def score(m):
+        q = q_ref[:, m * dh : (m + 1) * dh]
+        for b in range(n):
+            scores[m, :, b * tok : (b + 1) * tok] = lax.dot_general(
+                q, kv[b, 0, :, m * dh : (m + 1) * dh], (((1,), (1,)), ((), ())),
+                preferred_element_type=jnp.float32,
+            ) * scale
+
+    part = 64
+
+    def soften(i, carry):
+        at = pl.multiple_of(i * part, part)
+        key_pos = lax.broadcasted_iota(jnp.int32, (1, n * tok), 1)
+        key_block = key_pos // BLK
+        which = i // (BLK // part)
+        block = c * blocks_here + which
+        length = len_ref[0]
+        stride = [stride_ref[0, j] for j in range(NSTR)]
+        for g in range(1, blocks_here):
+            length = jnp.where(which == g, len_ref[g], length)
+            stride = [jnp.where(which == g, stride_ref[g, j], stride[j]) for j in range(NSTR)]
+        floor = block - length
+        ok = key_block > floor
+        for j in range(NSTR):
+            ok = ok | (key_block == stride[j])
+        for j in range(GLOB):
+            g = glob_ref[j]
+            ok = ok | ((key_block == g) & (key_block <= floor))
+        last = jnp.where(ok, key_pos, n * tok)
+        query = c * tok + at + lax.broadcasted_iota(jnp.int32, (part, 1), 0)
+        allowed = last <= query
+        maps = []
+        for m in range(2):
+            s = jnp.where(allowed, scores[m, pl.ds(at, part), :], MASKED)
+            e = jnp.exp(s - jnp.max(s, -1, keepdims=True))
+            maps.append((e, 1.0 / jnp.sum(e, -1, keepdims=True)))
+        (e1, r1), (e2, r2) = maps
+        probs[pl.ds(at, part), :] = (e1 * r1 - e2 * (mixing * r2)).astype(probs.dtype)
+        return carry
+
+    score(0)
+    score(1)
+    for d in range(1, nz):
+        w_side(-d)
+    lax.fori_loop(0, tok // part, soften, 0)
+    mixed = jnp.zeros((tok, width), jnp.float32)
+    for b in range(n):
+        mixed = mixed + jnp.dot(
+            probs[:, b * tok : (b + 1) * tok], kv[b, 1], preferred_element_type=jnp.float32
+        )
+    normed = mixed * lax.rsqrt(jnp.mean(mixed * mixed, -1, keepdims=True) + 1e-05) * (1.0 - lam_init)
+    mine[...] = normed.astype(mine.dtype)
+    trade = remote(mine, theirs, nm_s, nm_r, core)
+    trade.start()
+
+    def twin_at(d, here):
+        @pl.when((z + d < nz) & (z + d >= 0))
+        def _():
+            w_twin(2 * (z + d) + (x if here else 1 - x))
+
+    for d in range(1, nz):
+        twin_at(d, True)
+    twin_at(0, False)
+    for d in range(1, nz):
+        twin_at(-d, True)
+        twin_at(d, False)
+    for d in range(1, nz):
+        twin_at(-d, False)
+    trade.wait()
+
+    for j in range(nh):
+        for which in range(2):
+            swap_copy(h * nh + j, which).wait_recv()
+        block = None
+        for left, weight in ((mine, wown.at[h * nh + j]), (theirs, wother.at[j])):
+            piece = lax.dot_general(
+                left[...], weight[...], (((1,), (1,)), ((), ())), preferred_element_type=jnp.float32
+            ).astype(jnp.bfloat16).astype(jnp.float32)
+            block = piece if block is None else block + piece
+        obuf[j] = block.astype(obuf.dtype)
+        pltpu.make_async_copy(obuf.at[j], out_ref.at[:, pl.ds(j * rows, rows)], out_s.at[j]).start()
+
+    for b in range(n):
+        zb, same = b // 2, (b % 2) == x
+
+        @pl.when(same & has_up & (zb <= z))
+        def _(b=b):
+            kv_copy(b, kvu_s, up).wait_send()
+            w_copy(b, wu_s, up).wait_send()
+
+        @pl.when(same & ((zb < z) | ((zb == z) & (x == 0))))
+        def _(b=b):
+            kv_copy(b, kvx_s, side).wait_send()
+
+        @pl.when(same & has_down & (zb >= z))
+        def _(b=b):
+            w_copy(b, wd_s, down).wait_send()
+
+        @pl.when(same)
+        def _(b=b):
+            w_copy(b, wx_s, side).wait_send()
+
+        @pl.when(c != b)
+        def _(b=b):
+            y_copy(b, lo).wait_send()
+
+    for j in range(nh):
+        for which in range(2):
+            swap_copy((1 - h) * nh + j, which).wait_send()
+        pltpu.make_async_copy(obuf.at[j], out_ref.at[:, pl.ds(j * rows, rows)], out_s.at[j]).wait()
+
+
+def fused(queries, keys, values, lambda_vectors, out_weight, local_len, stride_keys, global_blocks):
+    n = lax.axis_size("ctx")
+    tok, _, width = queries.shape
+    rows = out_weight.shape[0]
+    nh = n // 2
+    vmem = pl.BlockSpec(memory_space=pltpu.VMEM)
+    smem = pl.BlockSpec(memory_space=pltpu.SMEM)
+    hbm = pl.BlockSpec(memory_space=pl.ANY)
+    dma = pltpu.SemaphoreType.DMA
+    bf16 = jnp.bfloat16
+    return pl.pallas_call(
+        functools.partial(kernel, n),
+        out_shape=jax.ShapeDtypeStruct((tok, nh * rows), bf16),
+        in_specs=[vmem, vmem, vmem, hbm, vmem, smem, smem, smem],
+        out_specs=hbm,
+        scratch_shapes=[
+            pltpu.VMEM((n, 2, tok, width), bf16),
+            pltpu.VMEM((n, rows, width), bf16),
+            pltpu.VMEM((nh, rows, width), bf16),
+            pltpu.VMEM((2, tok, n * tok), jnp.float32),
+            pltpu.VMEM((tok, n * tok), bf16),
+            pltpu.VMEM((tok, width), bf16),
+            pltpu.VMEM((tok, width), bf16),
+            pltpu.VMEM((nh, tok, rows), bf16),
+        ]
+        + [dma((n,)) for _ in range(9)]
+        + [dma((n,)), dma((n,)), dma, dma, dma, dma((nh,))],
+        compiler_params=pltpu.CompilerParams(
+            collective_id=0, has_side_effects=True, vmem_limit_bytes=40 * 2**20
+        ),
+    )(
+        queries.reshape(tok, width), keys.reshape(tok, width), values.reshape(tok, width),
+        out_weight, lambda_vectors, local_len, stride_keys, global_blocks,
+    )
+
+
 def solution(mesh):
     in_specs = (
         P(("groups", "ctx"), "head", None),
@@ -135,4 +461,14 @@
         P("groups"),
     )
     out_specs = P(("groups", "ctx"), "head")
-    return jax.shard_map(body, mesh=mesh, in_specs=in_specs, out_specs=out_specs, check_vma=False)
+    shape = mesh.shape
+
+    def layer(queries, *rest):
+        per_device = queries.shape[0] // (shape["groups"] * shape["ctx"])
+        score_bytes = 8 * per_device * per_device * shape["ctx"]
+        fits = score_bytes <= 8 * 2**20 and shape["groups"] == 2 and shape["head"] == 2
+        chosen = fused if fits and shape["ctx"] % 2 == 0 else body
+        mapped = jax.shard_map(chosen, mesh=mesh, in_specs=in_specs, out_specs=out_specs, check_vma=False)
+        return mapped(queries, *rest)
+
+    return layer

time: 197 us -> 76.1 us (0.39)
  waiting for transfers between devices: 145 us -> 0 us
  Pallas kernels: 0 us -> 68 us
  between operations: 25 us -> 0.02 us
  matrix products: 7.61 us -> 0 us
  starting transfers between devices: 7.36 us -> 0 us
  other arithmetic: 3.48 us -> 0 us
    pallas_call x0 -> x1, Pallas kernels: none -> 68 us  [fused(): pl.pallas_call(functools.partial(kernel, n), out_shape=jax.ShapeDtypeStru...]
    all_gather x1 -> x0, waiting for transfers between devices: 67.6 us -> none  [body(): lax.all_gather(out_weight, 'ctx', axis=0, tiled=True)]
    psum x1 -> x0, waiting for transfers between devices: 36.6 us -> none  [from_root(): return lax.psum(kept, axis)]
    ppermute x4 -> x0, waiting for transfers between devices: 27.4 us -> none  [shifted(): return lax.ppermute(shard, axis, pairs)]
    reduce_scatter x1 -> x0, waiting for transfers between devices: 12.6 us -> none  [body(): lax.psum_scatter(partials.astype(jnp.bfloat16), 'head', scatter_dimension...]
    dot_general x4 -> x0, matrix products: 7.61 us -> none  [the longest x1 5.48 us: body(): lax.dot_general(flat_heads, lax.all_gather(out_weight, 'ctx', axis=0, til...]
    ppermute x4 -> x0, starting transfers between devices: 7.25 us -> none  [shifted(): return lax.ppermute(shard, axis, pairs)]
    unnamed x19 -> x17, local copies, waits for them, and re-layouts: 3.86 us -> 7.74 us
  transfers between devices with their start and end apart: 7 -> 0, of which waited for: 6 -> 0; matrix products, arithmetic and copies ran while one was open for 4% -> 0% of each run, Pallas kernels for 0% -> 0%
where the time goes in v1:
time: 76.1 us; the launch traced here: 75.7 us
  Pallas kernels  68 us (89%)
  local copies, waits for them, and re-layouts  7.74 us (10%)
    pallas_call x1, Pallas kernels, fused(): pl.pallas_call(functools.partial(kernel, n), out_shape=jax.ShapeDtypeStru...  68 us
    unnamed x17, local copies, waits for them, and re-layouts  7.74 us

profile of v1, /device:TPU:24, one launch (start us, length us, event | category | flops | bytes accessed | tf_op | source)
XLA Modules:
  0.0 75.7 jit_solution(5992220067387709764)
XLA Ops:
  0.0 0.0 copy-start
  0.0 1.0 %copy-done = bf16[1024,256]{1,0:T(8,128)(2,1)S(1)} copy-done((bf16[1024,256]{1,0:T(8,128)(2,1)S(1)}, bf16[1024,256]{1,0:T(8,128)(2,1)}, u32[]{:S(2)}) %copy-start) | copy-done | bytes 524312
  1.0 0.0 copy-start.1
  1.0 0.9 %copy-done.1 = bf16[256,1,256]{2,0,1:T(8,128)(2,1)S(1)} copy-done((bf16[256,1,256]{2,0,1:T(8,128)(2,1)S(1)}, bf16[256,1,256]{2,0,1:T(8,128)(2,1)}, u32[]{:S(2)}) %copy-start.1) | copy-done | bytes 131096
  1.9 0.0 copy-start.2
  1.9 0.9 %copy-done.2 = bf16[256,1,256]{2,0,1:T(8,128)(2,1)S(1)} copy-done((bf16[256,1,256]{2,0,1:T(8,128)(2,1)S(1)}, bf16[256,1,256]{2,0,1:T(8,128)(2,1)}, u32[]{:S(2)}) %copy-start.2) | copy-done | bytes 131096
  2.9 0.0 copy-start.3
  2.9 0.9 %copy-done.3 = bf16[256,1,256]{2,0,1:T(8,128)(2,1)S(1)} copy-done((bf16[256,1,256]{2,0,1:T(8,128)(2,1)S(1)}, bf16[256,1,256]{2,0,1:T(8,128)(2,1)}, u32[]{:S(2)}) %copy-start.3) | copy-done | bytes 131096
  3.8 0.0 copy-start.4
  3.8 0.7 copy-done.4
  4.4 0.0 copy-start.5
  4.4 0.7 copy-done.5
  5.1 0.0 copy-start.6
  5.1 0.7 copy-done.6
  5.8 0.0 copy-start.7
  5.8 0.7 copy-done.7
  6.4 68.0 %shard_map.82 = bf16[256,4096]{1,0:T(8,128)(2,1)S(1)} custom-call(bf16[256,256]{1,0:T(8,128)(2,1)S(1)} %bitcast.3, bf16[256,256]{1,0:T(8,128)(2,1)S(1)} %bitcast.4, bf16[256,256]{1,0:T(8,128)(2,1)S(1)} %bitcast.5, bf16[1024,256]{1,0:T(8,128)(2,1)S(1)} %copy-done, f32[4,1,128]{2,1,0:T(1,128)S(1)} %copy-done.4, s32[2]{0:T(128)S(1)} %copy-done.6, ...), custom_call_target="tpu_custom_call" | custom-call | tf_op jit(solution)/shard_map/pallas_call | solution.py:426
  74.4 1.3 %copy.10 = bf16[256,4096]{1,0:T(8,128)(2,1)} copy(bf16[256,4096]{1,0:T(8,128)(2,1)S(1)} %shard_map.82) | data formatting | bytes 4194304
Async XLA Ops:
  0.0 1.0 %copy-start = (bf16[1024,256]{1,0:T(8,128)(2,1)S(1)}, bf16[1024,256]{1,0:T(8,128)(2,1)}, u32[]{:S(2)}) copy-start(bf16[1024,256]{1,0:T(8,128)(2,1)} %w_ref.1) | copy-start | bytes 1572868
  1.0 0.9 %copy-start.1 = (bf16[256,1,256]{2,0,1:T(8,128)(2,1)S(1)}, bf16[256,1,256]{2,0,1:T(8,128)(2,1)}, u32[]{:S(2)}) copy-start(bf16[256,1,256]{2,0,1:T(8,128)(2,1)} %param.8) | copy-start | bytes 393220
  1.9 0.9 %copy-start.2 = (bf16[256,1,256]{2,0,1:T(8,128)(2,1)S(1)}, bf16[256,1,256]{2,0,1:T(8,128)(2,1)}, u32[]{:S(2)}) copy-start(bf16[256,1,256]{2,0,1:T(8,128)(2,1)} %param.9) | copy-start | bytes 393220
  2.9 0.9 %copy-start.3 = (bf16[256,1,256]{2,0,1:T(8,128)(2,1)S(1)}, bf16[256,1,256]{2,0,1:T(8,128)(2,1)}, u32[]{:S(2)}) copy-start(bf16[256,1,256]{2,0,1:T(8,128)(2,1)} %param.10) | copy-start | bytes 393220
  3.8 0.7 copy-start.4
  4.4 0.7 copy-start.5
  5.1 0.7 copy-start.6
  5.8 0.7 copy-start.7

commit v2 on v1

--- a/solution.py
+++ b/solution.py
@@ -131,8 +131,8 @@
 
 
 def kernel(
-    n, q_ref, k_ref, v_ref, w_ref, lam_ref, len_ref, stride_ref, glob_ref, out_ref,
-    kv, wown, wother, scores, probs, mine, theirs, obuf,
+    n, q_hbm, k_ref, v_ref, w_ref, lam_ref, len_ref, stride_ref, glob_ref, out_ref,
+    q_ref, kv, wown, wother, scores, probs, mine, theirs, obuf,
     kvu_s, kvx_s, kv_r, wu_s, wd_s, wx_s, w_r, wy_s, wy_r, sw_s, sw_r, nm_s, nm_r, loc, out_s,
 ):
     tok, width = q_ref.shape
@@ -160,10 +160,14 @@
     def _():
         pl.semaphore_signal(barrier, inc=1, device_id=down, device_id_type=MESH_ID)
 
-    load = pltpu.make_async_copy(w_ref, wown.at[c], loc)
-    load.start()
-    kv[c, 0] = k_ref[...]
-    kv[c, 1] = v_ref[...]
+    loads = [
+        pltpu.make_async_copy(src, dst, loc.at[i])
+        for i, (src, dst) in enumerate(
+            ((k_ref, kv.at[c, 0]), (v_ref, kv.at[c, 1]), (w_ref, wown.at[c]), (q_hbm, q_ref))
+        )
+    ]
+    for load in loads:
+        load.start()
     pl.semaphore_wait(barrier, 3 + has_up.astype(jnp.int32) + has_down.astype(jnp.int32))
 
     def remote(src, dst, send, recv, to):
@@ -253,6 +257,9 @@
             b = 2 * (z - d) + 1 - x
             kv_copy(b, kvx_s, side).wait_recv()
 
+    loads[0].wait()
+    loads[1].wait()
+
     @pl.when(has_up)
     def _():
         kv_copy(c, kvu_s, up).start()
@@ -261,7 +268,7 @@
     def _():
         kv_copy(c, kvx_s, side).start()
 
-    load.wait()
+    loads[2].wait()
 
     @pl.when(has_down)
     def _():
@@ -284,13 +291,6 @@
     for d in range(1, nz):
         kv_up(d)
         w_down(d)
-    w_side(0)
-    for d in range(1, nz):
-        w_up(d)
-        w_side(d)
-    for d in range(nz):
-        kv_side(d)
-
     scale = 1.0 / math.sqrt(dh)
     lam_init = 0.8 - 0.6 * math.exp(-0.3 * (LAYER - 1))
     lam = [lam_ref[i] for i in range(4)]
@@ -341,11 +341,26 @@
         probs[pl.ds(at, part), :] = (e1 * r1 - e2 * (mixing * r2)).astype(probs.dtype)
         return carry
 
-    score(0)
-    score(1)
-    for d in range(1, nz):
-        w_side(-d)
-    lax.fori_loop(0, tok // part, soften, 0)
+    chunks = tok // part
+    done = 0
+    w_side(0)
+    for d in range(1, nz + 1):
+        if d < nz:
+            w_up(d)
+            w_side(d)
+        if d > 1:
+            w_side(1 - d)
+        if d == max(nz - 2, 1):
+            for far in range(nz):
+                kv_side(far)
+            loads[3].wait()
+            score(0)
+            score(1)
+        if d >= max(nz - 2, 1) and done < chunks:
+            soften(done, 0)
+            done += 1
+    for i in range(done, chunks):
+        soften(i, 0)
     mixed = jnp.zeros((tok, width), jnp.float32)
     for b in range(n):
         mixed = mixed + jnp.dot(
@@ -371,7 +386,8 @@
         twin_at(-d, False)
     trade.wait()
 
-    for j in range(nh):
+    for i in range(nh):
+        j = jnp.where(z >= nz // 2, nh - 1 - i, i)
         for which in range(2):
             swap_copy(h * nh + j, which).wait_recv()
         block = None
@@ -380,8 +396,9 @@
                 left[...], weight[...], (((1,), (1,)), ((), ())), preferred_element_type=jnp.float32
             ).astype(jnp.bfloat16).astype(jnp.float32)
             block = piece if block is None else block + piece
-        obuf[j] = block.astype(obuf.dtype)
-        pltpu.make_async_copy(obuf.at[j], out_ref.at[:, pl.ds(j * rows, rows)], out_s.at[j]).start()
+        obuf[i] = block.astype(obuf.dtype)
+        at = pl.multiple_of(j * rows, rows)
+        pltpu.make_async_copy(obuf.at[i], out_ref.at[:, pl.ds(at, rows)], out_s.at[i]).start()
 
     for b in range(n):
         zb, same = b // 2, (b % 2) == x
@@ -426,9 +443,10 @@
     return pl.pallas_call(
         functools.partial(kernel, n),
         out_shape=jax.ShapeDtypeStruct((tok, nh * rows), bf16),
-        in_specs=[vmem, vmem, vmem, hbm, vmem, smem, smem, smem],
+        in_specs=[hbm, hbm, hbm, hbm, vmem, smem, smem, smem],
         out_specs=hbm,
         scratch_shapes=[
+            pltpu.VMEM((tok, width), bf16),
             pltpu.VMEM((n, 2, tok, width), bf16),
             pltpu.VMEM((n, rows, width), bf16),
             pltpu.VMEM((nh, rows, width), bf16),
@@ -439,9 +457,9 @@
             pltpu.VMEM((nh, tok, rows), bf16),
         ]
         + [dma((n,)) for _ in range(9)]
-        + [dma((n,)), dma((n,)), dma, dma, dma, dma((nh,))],
+        + [dma((n,)), dma((n,)), dma, dma, dma((4,)), dma((nh,))],
         compiler_params=pltpu.CompilerParams(
-            collective_id=0, has_side_effects=True, vmem_limit_bytes=40 * 2**20
+            collective_id=0, has_side_effects=True, vmem_limit_bytes=60 * 2**20
         ),
     )(
         queries.reshape(tok, width), keys.reshape(tok, width), values.reshape(tok, width),

time: 76.1 us -> 72.3 us (0.950)
  local copies, waits for them, and re-layouts: 7.74 us -> 3.13 us
  Pallas kernels: 68 us -> 68.8 us
    unnamed x17 -> x1, local copies, waits for them, and re-layouts: 7.74 us -> 3.13 us
    pallas_call x1, Pallas kernels: 68 us -> 68.8 us  [fused(): pl.pallas_call(functools.partial(kernel, n), out_shape=jax.ShapeDtypeStru...]
where the time goes in v2:
time: 72.3 us; the launch traced here: 71.9 us
  Pallas kernels  68.8 us (95%)
  local copies, waits for them, and re-layouts  3.13 us (4%)
    pallas_call x1, Pallas kernels, fused(): pl.pallas_call(functools.partial(kernel, n), out_shape=jax.ShapeDtypeStru...  68.8 us
    unnamed x1, local copies, waits for them, and re-layouts  3.13 us

profile of v2, /device:TPU:24, one launch (start us, length us, event | category | flops | bytes accessed | tf_op | source)
XLA Modules:
  0.0 71.9 jit_solution(935622644378538019)
XLA Ops:
  0.0 68.8 %shard_map.82 = bf16[256,4096]{1,0:T(8,128)(2,1)} custom-call(bf16[256,256]{1,0:T(8,128)(2,1)} %bitcast.3, bf16[256,256]{1,0:T(8,128)(2,1)} %bitcast.4, bf16[256,256]{1,0:T(8,128)(2,1)} %bitcast.5, bf16[1024,256]{1,0:T(8,128)(2,1)} %w_ref.1, f32[4,1,128]{2,1,0:T(1,128)} %lam_ref.1, s32[2]{0:T(128)} %len_ref.1, s32[2,3]{1,0:T(2,128)} %stride_ref.1, s32[4]{0:T(128)} %glob_ref.1), custom_call_target="tpu_custom_call" | custom-call | tf_op jit(solution)/shard_map/pallas_call | solution.py:443
  68.8 3.1 %copy.10 = bf16[256,4096]{1,0:T(8,128)(2,1)} copy(bf16[256,4096]{1,0:T(8,128)(2,1)} %shard_map.82) | data formatting | bytes 4194304

commit v3 on v2

--- a/solution.py
+++ b/solution.py
@@ -291,6 +291,11 @@
     for d in range(1, nz):
         kv_up(d)
         w_down(d)
+        w_up(d)
+        w_side(d - 1)
+        if d > 1:
+            w_side(1 - d)
+
     scale = 1.0 / math.sqrt(dh)
     lam_init = 0.8 - 0.6 * math.exp(-0.3 * (LAYER - 1))
     lam = [lam_ref[i] for i in range(4)]
@@ -342,25 +347,16 @@
         return carry
 
     chunks = tok // part
-    done = 0
-    w_side(0)
-    for d in range(1, nz + 1):
-        if d < nz:
-            w_up(d)
-            w_side(d)
-        if d > 1:
-            w_side(1 - d)
-        if d == max(nz - 2, 1):
-            for far in range(nz):
-                kv_side(far)
-            loads[3].wait()
-            score(0)
-            score(1)
-        if d >= max(nz - 2, 1) and done < chunks:
-            soften(done, 0)
-            done += 1
-    for i in range(done, chunks):
+    w_side(nz - 1)
+    for far in range(nz):
+        kv_side(far)
+    loads[3].wait()
+    score(0)
+    score(1)
+    for i in range(chunks):
         soften(i, 0)
+        if i == chunks // 2 - 1:
+            w_side(1 - nz)
     mixed = jnp.zeros((tok, width), jnp.float32)
     for b in range(n):
         mixed = mixed + jnp.dot(
@@ -378,12 +374,12 @@
 
     for d in range(1, nz):
         twin_at(d, True)
-    twin_at(0, False)
-    for d in range(1, nz):
         twin_at(-d, True)
-        twin_at(d, False)
-    for d in range(1, nz):
-        twin_at(-d, False)
+        twin_at(d - 1, False)
+        if d > 1:
+            twin_at(1 - d, False)
+    twin_at(nz - 1, False)
+    twin_at(1 - nz, False)
     trade.wait()
 
     for i in range(nh):

time: 72.3 us -> 62.4 us (0.86)
  Pallas kernels: 68.8 us -> 59.1 us
    pallas_call x1, Pallas kernels: 68.8 us -> 59.1 us  [fused(): pl.pallas_call(functools.partial(kernel, n), out_shape=jax.ShapeDtypeStru...]
where the time goes in v3:
time: 62.4 us; the launch traced here: 62.2 us
  Pallas kernels  59.1 us (95%)
  local copies, waits for them, and re-layouts  3.13 us (5%)
    pallas_call x1, Pallas kernels, fused(): pl.pallas_call(functools.partial(kernel, n), out_shape=jax.ShapeDtypeStru...  59.1 us
    unnamed x1, local copies, waits for them, and re-layouts  3.13 us

profile of v3, /device:TPU:24, one launch (start us, length us, event | category | flops | bytes accessed | tf_op | source)
XLA Modules:
  0.0 62.2 jit_solution(5713386394944711278)
XLA Ops:
  0.0 59.1 %shard_map.82 = bf16[256,4096]{1,0:T(8,128)(2,1)} custom-call(bf16[256,256]{1,0:T(8,128)(2,1)} %bitcast.3, bf16[256,256]{1,0:T(8,128)(2,1)} %bitcast.4, bf16[256,256]{1,0:T(8,128)(2,1)} %bitcast.5, bf16[1024,256]{1,0:T(8,128)(2,1)} %w_ref.1, f32[4,1,128]{2,1,0:T(1,128)} %lam_ref.1, s32[2]{0:T(128)} %len_ref.1, s32[2,3]{1,0:T(2,128)} %stride_ref.1, s32[4]{0:T(128)} %glob_ref.1), custom_call_target="tpu_custom_call" | custom-call | tf_op jit(solution)/shard_map/pallas_call | solution.py:439
  59.1 3.1 %copy.10 = bf16[256,4096]{1,0:T(8,128)(2,1)} copy(bf16[256,4096]{1,0:T(8,128)(2,1)} %shard_map.82) | data formatting | bytes 4194304

commit v4 on v3

--- a/solution.py
+++ b/solution.py
@@ -133,7 +133,7 @@
 def kernel(
     n, q_hbm, k_ref, v_ref, w_ref, lam_ref, len_ref, stride_ref, glob_ref, out_ref,
     q_ref, kv, wown, wother, scores, probs, mine, theirs, obuf,
-    kvu_s, kvx_s, kv_r, wu_s, wd_s, wx_s, w_r, wy_s, wy_r, sw_s, sw_r, nm_s, nm_r, loc, out_s,
+    kvu_s, kvx_s, kv_r, wu_s, wd_s, wf_s, wx_s, w_r, wy_s, wy_r, sw_s, sw_r, nm_s, nm_r, loc, out_s,
 ):
     tok, width = q_ref.shape
     dh = width // 2
@@ -186,6 +186,10 @@
         piece = wown.at[b, pl.ds(start, half)]
         return remote(piece, piece, wy_s.at[b], wy_r.at[b], twin)
 
+    def far_copy(b):
+        piece = wown.at[b, pl.ds(hi, half)]
+        return remote(piece, piece, wf_s.at[b], wy_r.at[b], down)
+
     def swap_copy(b, which):
         start = pl.multiple_of(which * half, half)
         slot = b % nh
@@ -221,9 +225,15 @@
             def _():
                 w_copy(b, wd_s, down).start()
 
-            y_copy(b, lo).start()
             w_copy(b, wx_s, side).start()
             swap(b, y)
+            far_copy(b).wait_recv()
+
+            @pl.when(has_down)
+            def _():
+                far_copy(b).start()
+
+            swap(b, 1 - y)
 
     def w_up(d):
         @pl.when(z >= d)
@@ -236,7 +246,8 @@
                 w_copy(b, wu_s, up).start()
 
             y_copy(b, lo).start()
-            w_copy(b, wx_s, side).start()
+            if d < nz - 1:
+                w_copy(b, wx_s, side).start()
             swap(b, y)
 
     def w_side(d):
@@ -245,6 +256,11 @@
             b = 2 * (z + d) + 1 - x
             w_copy(b, wx_s, side).wait_recv()
             y_copy(b, lo).start()
+            if d == 2 - nz:
+                @pl.when(z == nz - 2)
+                def _():
+                    w_copy(b, wu_s, up).start()
+
             swap(b, y)
 
     def w_twin(b):
@@ -273,6 +289,7 @@
     @pl.when(has_down)
     def _():
         w_copy(c, wd_s, down).start()
+        far_copy(c).start()
 
     w_copy(c, wx_s, side).start()
 
@@ -373,7 +390,6 @@
             w_twin(2 * (z + d) + (x if here else 1 - x))
 
     for d in range(1, nz):
-        twin_at(d, True)
         twin_at(-d, True)
         twin_at(d - 1, False)
         if d > 1:
@@ -411,12 +427,18 @@
         @pl.when(same & has_down & (zb >= z))
         def _(b=b):
             w_copy(b, wd_s, down).wait_send()
-
-        @pl.when(same)
+            far_copy(b).wait_send()
+
+        @pl.when(same & ((z < nz - 1) | (zb > 0)))
         def _(b=b):
             w_copy(b, wx_s, side).wait_send()
 
-        @pl.when(c != b)
+        if zb == 0:
+            @pl.when(jnp.logical_not(same) & (z == nz - 2))
+            def _(b=b):
+                w_copy(b, wu_s, up).wait_send()
+
+        @pl.when((c != b) & jnp.logical_not(same & (zb > z)))
         def _(b=b):
             y_copy(b, lo).wait_send()
 
@@ -452,7 +474,7 @@
             pltpu.VMEM((tok, width), bf16),
             pltpu.VMEM((nh, tok, rows), bf16),
         ]
-        + [dma((n,)) for _ in range(9)]
+        + [dma((n,)) for _ in range(10)]
         + [dma((n,)), dma((n,)), dma, dma, dma((4,)), dma((nh,))],
         compiler_params=pltpu.CompilerParams(
             collective_id=0, has_side_effects=True, vmem_limit_bytes=60 * 2**20
@@ -481,7 +503,7 @@
         per_device = queries.shape[0] // (shape["groups"] * shape["ctx"])
         score_bytes = 8 * per_device * per_device * shape["ctx"]
         fits = score_bytes <= 8 * 2**20 and shape["groups"] == 2 and shape["head"] == 2
-        chosen = fused if fits and shape["ctx"] % 2 == 0 else body
+        chosen = fused if fits and shape["ctx"] % 2 == 0 and shape["ctx"] >= 4 else body
         mapped = jax.shard_map(chosen, mesh=mesh, in_specs=in_specs, out_specs=out_specs, check_vma=False)
         return mapped(queries, *rest)
 

time: 62.4 us -> 62.4 us (level)
  no operation moved by 1% of the time
where the time goes in v4:
time: 62.4 us; the launch traced here: 62.3 us
  Pallas kernels  59.1 us (95%)
  local copies, waits for them, and re-layouts  3.13 us (5%)
    pallas_call x1, Pallas kernels, fused(): pl.pallas_call(functools.partial(kernel, n), out_shape=jax.ShapeDtypeStru...  59.1 us
    unnamed x1, local copies, waits for them, and re-layouts  3.13 us

profile of v4, /device:TPU:24, one launch (start us, length us, event | category | flops | bytes accessed | tf_op | source)
XLA Modules:
  0.0 62.3 jit_solution(6531143290636390513)
XLA Ops:
  0.0 59.1 %shard_map.82 = bf16[256,4096]{1,0:T(8,128)(2,1)} custom-call(bf16[256,256]{1,0:T(8,128)(2,1)} %bitcast.3, bf16[256,256]{1,0:T(8,128)(2,1)} %bitcast.4, bf16[256,256]{1,0:T(8,128)(2,1)} %bitcast.5, bf16[1024,256]{1,0:T(8,128)(2,1)} %w_ref.1, f32[4,1,128]{2,1,0:T(1,128)} %lam_ref.1, s32[2]{0:T(128)} %len_ref.1, s32[2,3]{1,0:T(2,128)} %stride_ref.1, s32[4]{0:T(128)} %glob_ref.1), custom_call_target="tpu_custom_call" | custom-call | tf_op jit(solution)/shard_map/pallas_call | solution.py:461
  59.1 3.1 %copy.10 = bf16[256,4096]{1,0:T(8,128)(2,1)} copy(bf16[256,4096]{1,0:T(8,128)(2,1)} %shard_map.82) | data formatting | bytes 4194304

commit v5 on v3

--- a/solution.py
+++ b/solution.py
@@ -11,6 +11,7 @@
 BLK = 128
 NSTR = 3
 GLOB = 4
+PIECES = 2
 LAYER = 12
 
 
@@ -133,20 +134,23 @@
 def kernel(
     n, q_hbm, k_ref, v_ref, w_ref, lam_ref, len_ref, stride_ref, glob_ref, out_ref,
     q_ref, kv, wown, wother, scores, probs, mine, theirs, obuf,
-    kvu_s, kvx_s, kv_r, wu_s, wd_s, wx_s, w_r, wy_s, wy_r, sw_s, sw_r, nm_s, nm_r, loc, out_s,
+    kvu_s, kvx_s, kv_r, wu_s, wd_s, wf_s, wx_s, w_r, wy_s, wy_r, sw_s, sw_r, nm_s, nm_r, loc, out_s,
 ):
     tok, width = q_ref.shape
     dh = width // 2
     rows = w_ref.shape[0]
     half = rows // 2
+    size = half // PIECES
     nz, nh = n // 2, n // 2
     y, c, h = lax.axis_index("groups"), lax.axis_index("ctx"), lax.axis_index("head")
     z, x = c // 2, c % 2
     has_up, has_down = z + 1 < nz, z >= 1
     up, down, side = {"ctx": c + 2}, {"ctx": c - 2}, {"ctx": c + 1 - 2 * x}
     twin, core = {"groups": 1 - y}, {"head": 1 - h}
-    lo = pl.multiple_of(y * half, half)
-    hi = pl.multiple_of((1 - y) * half, half)
+    lo, hi = y, 1 - y
+
+    def rows_of(which, p):
+        return pl.ds(pl.multiple_of(which * half + p * size, size), size)
 
     barrier = pltpu.get_barrier_semaphore()
     for to in (side, twin, core):
@@ -178,26 +182,29 @@
     def kv_copy(b, send, to):
         return remote(kv.at[b], kv.at[b], send.at[b], kv_r.at[b], to)
 
-    def w_copy(b, send, to):
-        piece = wown.at[b, pl.ds(lo, half)]
-        return remote(piece, piece, send.at[b], w_r.at[b], to)
-
-    def y_copy(b, start):
-        piece = wown.at[b, pl.ds(start, half)]
-        return remote(piece, piece, wy_s.at[b], wy_r.at[b], twin)
-
-    def swap_copy(b, which):
-        start = pl.multiple_of(which * half, half)
+    def w_copy(b, p, send, to):
+        piece = wown.at[b, rows_of(lo, p)]
+        return remote(piece, piece, send.at[b, p], w_r.at[b, p], to)
+
+    def y_copy(b, p, which):
+        piece = wown.at[b, rows_of(which, p)]
+        return remote(piece, piece, wy_s.at[b, p], wy_r.at[b, p], twin)
+
+    def far_copy(b, p):
+        piece = wown.at[b, rows_of(hi, p)]
+        return remote(piece, piece, wf_s.at[b, p], wy_r.at[b, p], down)
+
+    def swap_copy(b, which, p):
         slot = b % nh
         return remote(
-            wown.at[b, pl.ds(start, half)], wother.at[slot, pl.ds(start, half)],
-            sw_s.at[2 * slot + which], sw_r.at[2 * slot + which], core,
+            wown.at[b, rows_of(which, p)], wother.at[slot, rows_of(which, p)],
+            sw_s.at[2 * slot + which, p], sw_r.at[2 * slot + which, p], core,
         )
 
-    def swap(b, which):
+    def swap(b, which, p):
         @pl.when(b // nh == 1 - h)
         def _():
-            swap_copy(b, which).start()
+            swap_copy(b, which, p).start()
 
     def kv_up(d):
         @pl.when(z >= d)
@@ -215,47 +222,76 @@
         @pl.when(z + d < nz)
         def _():
             b = c + 2 * d
-            w_copy(b, wd_s, down).wait_recv()
-
-            @pl.when(has_down)
-            def _():
-                w_copy(b, wd_s, down).start()
-
-            y_copy(b, lo).start()
-            w_copy(b, wx_s, side).start()
-            swap(b, y)
+            for p in range(PIECES):
+                w_copy(b, p, wd_s, down).wait_recv()
+
+                @pl.when(has_down)
+                def _():
+                    w_copy(b, p, wd_s, down).start()
+
+                w_copy(b, p, wx_s, side).start()
+                swap(b, lo, p)
+            for p in range(PIECES):
+                far_copy(b, p).wait_recv()
+
+                @pl.when(has_down)
+                def _():
+                    far_copy(b, p).start()
+
+                swap(b, hi, p)
 
     def w_up(d):
         @pl.when(z >= d)
         def _():
             b = c - 2 * d
-            w_copy(b, wu_s, up).wait_recv()
-
-            @pl.when(has_up)
-            def _():
-                w_copy(b, wu_s, up).start()
-
-            y_copy(b, lo).start()
-            w_copy(b, wx_s, side).start()
-            swap(b, y)
+            for p in range(PIECES):
+                w_copy(b, p, wu_s, up).wait_recv()
+
+                @pl.when(has_up)
+                def _():
+                    w_copy(b, p, wu_s, up).start()
+
+                y_copy(b, p, lo).start()
+                if d < nz - 1:
+                    w_copy(b, p, wx_s, side).start()
+                swap(b, lo, p)
 
     def w_side(d):
         @pl.when((z + d < nz) & (z + d >= 0))
         def _():
             b = 2 * (z + d) + 1 - x
-            w_copy(b, wx_s, side).wait_recv()
-            y_copy(b, lo).start()
-            swap(b, y)
+            for p in range(PIECES):
+                w_copy(b, p, wx_s, side).wait_recv()
+                y_copy(b, p, lo).start()
+                if d == 2 - nz:
+                    @pl.when(z == nz - 2)
+                    def _():
+                        w_copy(b, p, wu_s, up).start()
+
+                swap(b, lo, p)
 
     def w_twin(b):
-        y_copy(b, hi).wait_recv()
-        swap(b, 1 - y)
+        for p in range(PIECES):
+            y_copy(b, p, hi).wait_recv()
+            swap(b, hi, p)
 
     def kv_side(d):
         @pl.when((z >= d) & ((d > 0) | (x == 1)))
         def _():
             b = 2 * (z - d) + 1 - x
             kv_copy(b, kvx_s, side).wait_recv()
+
+    loads[2].wait()
+    for p in range(PIECES):
+        @pl.when(has_up)
+        def _():
+            w_copy(c, p, wu_s, up).start()
+
+        w_copy(c, p, wx_s, side).start()
+
+        @pl.when(has_down)
+        def _():
+            w_copy(c, p, wd_s, down).start()
 
     loads[0].wait()
     loads[1].wait()
@@ -268,20 +304,13 @@
     def _():
         kv_copy(c, kvx_s, side).start()
 
-    loads[2].wait()
-
-    @pl.when(has_down)
-    def _():
-        w_copy(c, wd_s, down).start()
-
-    w_copy(c, wx_s, side).start()
-
-    @pl.when(has_up)
-    def _():
-        w_copy(c, wu_s, up).start()
-
-    swap(c, 0)
-    swap(c, 1)
+    for p in range(PIECES):
+        @pl.when(has_down)
+        def _():
+            far_copy(c, p).start()
+
+        swap(c, 0, p)
+        swap(c, 1, p)
 
     for b in range(1, n):
         @pl.when(c < b)
@@ -289,12 +318,12 @@
             kv[b] = jnp.zeros(kv.shape[1:], kv.dtype)
 
     for d in range(1, nz):
-        kv_up(d)
-        w_down(d)
         w_up(d)
         w_side(d - 1)
         if d > 1:
             w_side(1 - d)
+        kv_up(d)
+        w_down(d)
 
     scale = 1.0 / math.sqrt(dh)
     lam_init = 0.8 - 0.6 * math.exp(-0.3 * (LAYER - 1))
@@ -373,7 +402,6 @@
             w_twin(2 * (z + d) + (x if here else 1 - x))
 
     for d in range(1, nz):
-        twin_at(d, True)
         twin_at(-d, True)
         twin_at(d - 1, False)
         if d > 1:
@@ -385,7 +413,8 @@
     for i in range(nh):
         j = jnp.where(z >= nz // 2, nh - 1 - i, i)
         for which in range(2):
-            swap_copy(h * nh + j, which).wait_recv()
+            for p in range(PIECES):
+                swap_copy(h * nh + j, which, p).wait_recv()
         block = None
         for left, weight in ((mine, wown.at[h * nh + j]), (theirs, wother.at[j])):
             piece = lax.dot_general(
@@ -402,7 +431,8 @@
         @pl.when(same & has_up & (zb <= z))
         def _(b=b):
             kv_copy(b, kvu_s, up).wait_send()
-            w_copy(b, wu_s, up).wait_send()
+            for p in range(PIECES):
+                w_copy(b, p, wu_s, up).wait_send()
 
         @pl.when(same & ((zb < z) | ((zb == z) & (x == 0))))
         def _(b=b):
@@ -410,19 +440,31 @@
 
         @pl.when(same & has_down & (zb >= z))
         def _(b=b):
-            w_copy(b, wd_s, down).wait_send()
-
-        @pl.when(same)
+            for p in range(PIECES):
+                w_copy(b, p, wd_s, down).wait_send()
+            for p in range(PIECES):
+                far_copy(b, p).wait_send()
+
+        @pl.when(same & ((z < nz - 1) | (zb > 0)))
         def _(b=b):
-            w_copy(b, wx_s, side).wait_send()
-
-        @pl.when(c != b)
+            for p in range(PIECES):
+                w_copy(b, p, wx_s, side).wait_send()
+
+        if zb == 0:
+            @pl.when(jnp.logical_not(same) & (z == nz - 2))
+            def _(b=b):
+                for p in range(PIECES):
+                    w_copy(b, p, wu_s, up).wait_send()
+
+        @pl.when((c != b) & jnp.logical_not(same & (zb > z)))
         def _(b=b):
-            y_copy(b, lo).wait_send()
+            for p in range(PIECES):
+                y_copy(b, p, lo).wait_send()
 
     for j in range(nh):
         for which in range(2):
-            swap_copy((1 - h) * nh + j, which).wait_send()
+            for p in range(PIECES):
+                swap_copy((1 - h) * nh + j, which, p).wait_send()
         pltpu.make_async_copy(obuf.at[j], out_ref.at[:, pl.ds(j * rows, rows)], out_s.at[j]).wait()
 
 
@@ -452,8 +494,10 @@
             pltpu.VMEM((tok, width), bf16),
             pltpu.VMEM((nh, tok, rows), bf16),
         ]
-        + [dma((n,)) for _ in range(9)]
-        + [dma((n,)), dma((n,)), dma, dma, dma((4,)), dma((nh,))],
+        + [dma((n,))] * 3
+        + [dma((n, PIECES))] * 7
+        + [dma((n, PIECES))] * 2
+        + [dma, dma, dma((4,)), dma((nh,))],
         compiler_params=pltpu.CompilerParams(
             collective_id=0, has_side_effects=True, vmem_limit_bytes=60 * 2**20
         ),
@@ -481,7 +525,7 @@
         per_device = queries.shape[0] // (shape["groups"] * shape["ctx"])
         score_bytes = 8 * per_device * per_device * shape["ctx"]
         fits = score_bytes <= 8 * 2**20 and shape["groups"] == 2 and shape["head"] == 2
-        chosen = fused if fits and shape["ctx"] % 2 == 0 else body
+        chosen = fused if fits and shape["ctx"] % 2 == 0 and shape["ctx"] >= 4 else body
         mapped = jax.shard_map(chosen, mesh=mesh, in_specs=in_specs, out_specs=out_specs, check_vma=False)
         return mapped(queries, *rest)
 

time: 62.4 us -> 61 us (0.978)
  Pallas kernels: 59.1 us -> 57.7 us
    pallas_call x1, Pallas kernels: 59.1 us -> 57.7 us  [fused(): pl.pallas_call(functools.partial(kernel, n), out_shape=jax.ShapeDtypeStru...]
where the time goes in v5:
time: 61 us; the launch traced here: 60.8 us
  Pallas kernels  57.7 us (95%)
  local copies, waits for them, and re-layouts  3.13 us (5%)
    pallas_call x1, Pallas kernels, fused(): pl.pallas_call(functools.partial(kernel, n), out_shape=jax.ShapeDtypeStru...  57.7 us
    unnamed x1, local copies, waits for them, and re-layouts  3.13 us

profile of v5, /device:TPU:24, one launch (start us, length us, event | category | flops | bytes accessed | tf_op | source)
XLA Modules:
  0.0 60.8 jit_solution(3417042082786752107)
XLA Ops:
  0.0 57.7 %shard_map.82 = bf16[256,4096]{1,0:T(8,128)(2,1)} custom-call(bf16[256,256]{1,0:T(8,128)(2,1)} %bitcast.3, bf16[256,256]{1,0:T(8,128)(2,1)} %bitcast.4, bf16[256,256]{1,0:T(8,128)(2,1)} %bitcast.5, bf16[1024,256]{1,0:T(8,128)(2,1)} %w_ref.1, f32[4,1,128]{2,1,0:T(1,128)} %lam_ref.1, s32[2]{0:T(128)} %len_ref.1, s32[2,3]{1,0:T(2,128)} %stride_ref.1, s32[4]{0:T(128)} %glob_ref.1), custom_call_target="tpu_custom_call" | custom-call | tf_op jit(solution)/shard_map/pallas_call | solution.py:481
  57.7 3.1 %copy.10 = bf16[256,4096]{1,0:T(8,128)(2,1)} copy(bf16[256,4096]{1,0:T(8,128)(2,1)} %shard_map.82) | data formatting | bytes 4194304

commit v6 on v5

--- a/solution.py
+++ b/solution.py
@@ -231,6 +231,11 @@
 
                 w_copy(b, p, wx_s, side).start()
                 swap(b, lo, p)
+
+    def far_down(d):
+        @pl.when(z + d < nz)
+        def _():
+            b = c + 2 * d
             for p in range(PIECES):
                 far_copy(b, p).wait_recv()
 
@@ -318,12 +323,16 @@
             kv[b] = jnp.zeros(kv.shape[1:], kv.dtype)
 
     for d in range(1, nz):
+        w_down(d)
+        if d > 1:
+            kv_up(d)
         w_up(d)
+        if d == 1:
+            kv_up(d)
         w_side(d - 1)
         if d > 1:
             w_side(1 - d)
-        kv_up(d)
-        w_down(d)
+        far_down(d)
 
     scale = 1.0 / math.sqrt(dh)
     lam_init = 0.8 - 0.6 * math.exp(-0.3 * (LAYER - 1))
@@ -406,12 +415,14 @@
         twin_at(d - 1, False)
         if d > 1:
             twin_at(1 - d, False)
-    twin_at(nz - 1, False)
-    twin_at(1 - nz, False)
     trade.wait()
 
     for i in range(nh):
-        j = jnp.where(z >= nz // 2, nh - 1 - i, i)
+        if i == nh - 1:
+            twin_at(nz - 1, False)
+            twin_at(1 - nz, False)
+        pair = jnp.where(z >= nz // 2, nh // 2 - 1 - i // 2, i // 2)
+        j = 2 * pair + (x if i % 2 == 0 else 1 - x)
         for which in range(2):
             for p in range(PIECES):
                 swap_copy(h * nh + j, which, p).wait_recv()
@@ -525,7 +536,7 @@
         per_device = queries.shape[0] // (shape["groups"] * shape["ctx"])
         score_bytes = 8 * per_device * per_device * shape["ctx"]
         fits = score_bytes <= 8 * 2**20 and shape["groups"] == 2 and shape["head"] == 2
-        chosen = fused if fits and shape["ctx"] % 2 == 0 and shape["ctx"] >= 4 else body
+        chosen = fused if fits and shape["ctx"] % 4 == 0 else body
         mapped = jax.shard_map(chosen, mesh=mesh, in_specs=in_specs, out_specs=out_specs, check_vma=False)
         return mapped(queries, *rest)
 

time: 61 us -> 61.4 us (level)
  no operation moved by 1% of the time
where the time goes in v6:
time: 61.4 us; the launch traced here: 61.2 us
  Pallas kernels  58.1 us (95%)
  local copies, waits for them, and re-layouts  3.13 us (5%)
    pallas_call x1, Pallas kernels, fused(): pl.pallas_call(functools.partial(kernel, n), out_shape=jax.ShapeDtypeStru...  58.1 us
    unnamed x1, local copies, waits for them, and re-layouts  3.13 us

profile of v6, /device:TPU:24, one launch (start us, length us, event | category | flops | bytes accessed | tf_op | source)
XLA Modules:
  0.0 61.2 jit_solution(6176523024727941802)
XLA Ops:
  0.0 58.1 %shard_map.82 = bf16[256,4096]{1,0:T(8,128)(2,1)} custom-call(bf16[256,256]{1,0:T(8,128)(2,1)} %bitcast.3, bf16[256,256]{1,0:T(8,128)(2,1)} %bitcast.4, bf16[256,256]{1,0:T(8,128)(2,1)} %bitcast.5, bf16[1024,256]{1,0:T(8,128)(2,1)} %w_ref.1, f32[4,1,128]{2,1,0:T(1,128)} %lam_ref.1, s32[2]{0:T(128)} %len_ref.1, s32[2,3]{1,0:T(2,128)} %stride_ref.1, s32[4]{0:T(128)} %glob_ref.1), custom_call_target="tpu_custom_call" | custom-call | tf_op jit(solution)/shard_map/pallas_call | solution.py:492
  58.1 3.1 %copy.10 = bf16[256,4096]{1,0:T(8,128)(2,1)} copy(bf16[256,4096]{1,0:T(8,128)(2,1)} %shard_map.82) | data formatting | bytes 4194304

commit v7 on v6

--- a/solution.py
+++ b/solution.py
@@ -324,14 +324,11 @@
 
     for d in range(1, nz):
         w_down(d)
-        if d > 1:
-            kv_up(d)
         w_up(d)
-        if d == 1:
-            kv_up(d)
         w_side(d - 1)
         if d > 1:
             w_side(1 - d)
+        kv_up(d)
         far_down(d)
 
     scale = 1.0 / math.sqrt(dh)
@@ -393,7 +390,7 @@
     score(1)
     for i in range(chunks):
         soften(i, 0)
-        if i == chunks // 2 - 1:
+        if i == 0:
             w_side(1 - nz)
     mixed = jnp.zeros((tok, width), jnp.float32)
     for b in range(n):

time: 61.4 us -> 57.1 us (0.930)
  Pallas kernels: 58.1 us -> 53.8 us
    pallas_call x1, Pallas kernels: 58.1 us -> 53.8 us  [fused(): pl.pallas_call(functools.partial(kernel, n), out_shape=jax.ShapeDtypeStru...]
where the time goes in v7:
time: 57.1 us; the launch traced here: 56.9 us
  Pallas kernels  53.8 us (94%)
  local copies, waits for them, and re-layouts  3.13 us (5%)
    pallas_call x1, Pallas kernels, fused(): pl.pallas_call(functools.partial(kernel, n), out_shape=jax.ShapeDtypeStru...  53.8 us
    unnamed x1, local copies, waits for them, and re-layouts  3.13 us

profile of v7, /device:TPU:24, one launch (start us, length us, event | category | flops | bytes accessed | tf_op | source)
XLA Modules:
  0.0 56.9 jit_solution(3554727530866895492)
XLA Ops:
  0.0 53.8 %shard_map.82 = bf16[256,4096]{1,0:T(8,128)(2,1)} custom-call(bf16[256,256]{1,0:T(8,128)(2,1)} %bitcast.3, bf16[256,256]{1,0:T(8,128)(2,1)} %bitcast.4, bf16[256,256]{1,0:T(8,128)(2,1)} %bitcast.5, bf16[1024,256]{1,0:T(8,128)(2,1)} %w_ref.1, f32[4,1,128]{2,1,0:T(1,128)} %lam_ref.1, s32[2]{0:T(128)} %len_ref.1, s32[2,3]{1,0:T(2,128)} %stride_ref.1, s32[4]{0:T(128)} %glob_ref.1), custom_call_target="tpu_custom_call" | custom-call | tf_op jit(solution)/shard_map/pallas_call | solution.py:489
  53.8 3.1 %copy.10 = bf16[256,4096]{1,0:T(8,128)(2,1)} copy(bf16[256,4096]{1,0:T(8,128)(2,1)} %shard_map.82) | data formatting | bytes 4194304
